TPU v7x, 512 devices: a whole 4x8x8 slice. The times are simulated.
512 devices in a mesh: mem: 16 (over y_lo, z), sp: 32 (over y_hi, x, core).
Axes of the slice: x: 4, y: 8 (y_hi: 4, y_lo: 2; y = y_hi * 2 + y_lo), z: 8, core: 2. Of those that a mesh axis runs over, the one named last changes fastest.
Arguments:
- grad_image: bfloat16 [16, 256, 128, 512], P('mem', 'sp'), may hold values from -6 to 6
- conv_weight: bfloat16 [3, 3, 512, 512], P(None, None, 'sp', 'mem'), may hold values from -0.09375 to 0.09375
- input_weight: bfloat16 [3, 3, 16, 512], P(None, None, None, 'sp'), may hold values from -0.09375 to 0.09375
- hidden: bfloat16 [16, 2048, 2432], P('mem', 'sp'), may hold values from -6 to 6
- shift: float32 [16, 2432], P('mem'), may hold values from -3 to 3
- scale: float32 [16, 2432], P('mem'), may hold values from -3 to 3
- final_weight: bfloat16 [2432, 64], P('sp'), may hold values from -0.75 to 0.75
Outputs:
- grad_hidden: bfloat16 [16, 2048, 2432], P('mem', 'sp')
- grad_final: float32 [2432, 64], P('sp')
- grad_scale: float32 [16, 2432], P('mem')
- grad_shift: float32 [16, 2432], P('mem')
All inputs are finite; a program needn't handle non-finite values.
Results may differ from a plain program's by a relative error of at most 0.011.
Values may be sent and summed in bfloat16 or wider, within the bound.
A program may use at most 64 MiB of HBM per device.

v0:
```python
import jax
import jax.numpy as jnp
from jax import lax
from jax.sharding import PartitionSpec as P


def with_halo(block, sides, width):
    for axis, dim in sides:
        count = lax.axis_size(axis)
        forward = [(i, i + 1) for i in range(count - 1)]
        backward = [(target, source) for source, target in forward]
        low = lax.ppermute(
            lax.slice_in_dim(block, block.shape[dim] - width, None, axis=dim), axis, forward
        )
        high = lax.ppermute(lax.slice_in_dim(block, 0, width, axis=dim), axis, backward)
        block = jnp.concatenate([low, block, high], axis=dim)
    return block


def shifted(padded, row_tap, col_tap, height, breadth):
    return padded[:, 2 - row_tap : 2 - row_tap + height, 2 - col_tap : 2 - col_tap + breadth, :]


def pooling(field):
    count, height, breadth, depth = field.shape
    return field.reshape(count, height // 2, 2, breadth // 2, 2, depth).sum(axis=(2, 4))


def pad_columns(field):
    return jnp.pad(field, ((0, 0), (0, 0), (1, 1), (0, 0)))


def per_device(grad_image, conv_weight, input_weight, hidden, shift, scale, final_weight):
    count, height, breadth, depth = grad_image.shape
    edged = with_halo(grad_image, (("sp", 1),), 1)
    padded = pad_columns(edged)
    partial_weight = lax.all_gather(conv_weight, "mem", axis=3, tiled=True)
    piece = lax.all_gather(partial_weight, "sp", axis=2, tiled=True)
    total = jnp.zeros((count, height, breadth, piece.shape[2]), jnp.float32)
    for by_row_tap in range(3):
        for by_col_tap in range(3):
            by_window = shifted(padded, by_row_tap, by_col_tap, height, breadth)
            total = total + jnp.einsum(
                "mrwj,kj->mrwk",
                by_window,
                piece[by_row_tap, by_col_tap],
                preferred_element_type=jnp.float32,
            )
    pooled = pooling(total)
    whole_input, whole_final = (
        lax.all_gather(input_weight, "sp", axis=3, tiled=True),
        lax.all_gather(final_weight, "sp", axis=0, tiled=True),
    )
    input_exact = whole_input.astype(jnp.float32)
    pooled_edged = pad_columns(with_halo(pooled, (("sp", 1),), 1))
    half_height = height // 2
    half_breadth = breadth // 2
    latent_channels = whole_input.shape[2]
    grad_latent = jnp.zeros((count, half_height, half_breadth, latent_channels), jnp.float32)
    for row_tap in range(3):
        for col_tap in range(3):
            window = shifted(pooled_edged, row_tap, col_tap, half_height, half_breadth)
            grad_latent = grad_latent + jnp.einsum(
                "mrwc,lc->mrwl",
                window,
                input_exact[row_tap, col_tap],
                precision=lax.Precision.HIGHEST,
            )
    grad_latent = grad_latent / 1.5305
    grad_tokens = grad_latent.reshape(
        count, height // 4, 2, breadth // 4, 2, latent_channels
    ).transpose(0, 1, 3, 2, 4, 5)
    grad_tokens = grad_tokens.reshape(
        count, height // 4 * (breadth // 4), 4 * latent_channels
    ).astype(jnp.bfloat16)
    values = hidden.astype(jnp.float32)
    centred = values - jnp.mean(values, axis=-1, keepdims=True)
    inverse = lax.rsqrt(jnp.mean(centred * centred, axis=-1, keepdims=True) + 1e-06)
    normed = centred * inverse
    factor = (1.0 + scale)[:, None, :]
    modulated = (normed * factor + shift[:, None, :]).astype(jnp.bfloat16)
    grad_mod = jnp.einsum(
        "mtp,dp->mtd", grad_tokens, whole_final, preferred_element_type=jnp.float32
    )
    grad_shift, grad_scale = lax.psum(
        (jnp.sum(grad_mod, axis=1), jnp.sum(grad_mod * normed, axis=1)), "sp"
    )
    scaled = grad_mod * factor
    grad_hidden = (
        scaled
        - jnp.mean(scaled, axis=-1, keepdims=True)
        - normed * jnp.mean(scaled * normed, axis=-1, keepdims=True)
    ) * inverse
    local_rows = lax.psum_scatter(
        jnp.einsum("mtd,mtp->dp", modulated, grad_tokens, preferred_element_type=jnp.float32),
        "sp",
        scatter_dimension=0,
        tiled=True,
    )
    grad_final = lax.psum(local_rows, "mem")
    return (grad_hidden.astype(jnp.bfloat16), grad_final, grad_scale, grad_shift)


def solution(mesh):
    placed = (
        P("mem", "sp", None, None),
        P(None, None, "sp", "mem"),
        P(None, None, None, "sp"),
        P("mem", "sp", None),
        P("mem", None),
        P("mem", None),
        P("sp", None),
    )
    return jax.shard_map(
        per_device,
        mesh=mesh,
        in_specs=placed,
        out_specs=(P("mem", "sp", None), P("sp", None), P("mem", None), P("mem", None)),
        check_vma=False,
    )
```

profile of v0, /device:TPU:8, one launch (start us, length us, event | category | flops | bytes accessed | tf_op | source)
XLA Modules:
  0.0 568.8 jit_solution(9357675494703975293)
XLA Ops:
  7.2 1.0 copy.14
  8.2 48.1 %all_gather.12 = bf16[3,3,16,512]{2,1,0,3:T(4,128)(2,1)S(1)} all-gather(bf16[3,3,16,32]{2,1,0,3:T(4,128)(2,1)S(1)} %copy.14), channel_id=1, replica_groups=mesh['mem'=16,'sp'=32] {'mem'}, dimensions={3}, use_global_device_ids=true | all-gather | bytes 156672 | tf_op jit(solution)/shard_map/all_gather | solution.py:37
  56.3 2.0 copy.15
  58.5 1.3 collective-permute-start
  59.8 1.3 collective-permute-start.1
  61.2 59.4 %all_gather.14 = bf16[3,3,16,512]{2,1,0,3:T(4,128)(2,1)S(1)} all-gather(bf16[3,3,16,16]{2,1,0,3:T(4,128)(2,1)S(1)} %copy.16), channel_id=1, replica_groups=mesh['mem'=16,'sp'=32] {'sp'}, dimensions={3}, use_global_device_ids=true | all-gather | bytes 152064 | tf_op jit(solution)/shard_map/all_gather | solution.py:51
  121.0 2.9 fusion.68
  124.3 1.4 all-gather.3.cloned.1.call-done
  125.6 1.9 fusion.13
  127.6 1.8 fusion.14
  129.4 0.7 fusion.15
  130.1 0.7 fusion.16
  130.9 0.7 fusion.21
  131.6 0.7 fusion.9
  134.0 1.2 add_add_fusion
  135.3 2.3 reshape.178
  137.6 3.2 reduce_sum.69
  141.6 2.8 collective-permute-start.2
  144.3 1.3 collective-permute-start.3
  145.6 46.9 %all-gather = bf16[32,76,64]{1,2,0:T(8,128)(2,1)S(1)} all-gather(bf16[1,76,64]{1,2,0:T(8,128)(2,1)S(1)} %bitcast.171), channel_id=1, replica_groups=mesh['mem'=16,'sp'=32] {'sp'}, dimensions={0}, use_global_device_ids=true | all-gather | bytes 321024 | tf_op jit(solution)/shard_map/all_gather | solution.py:52
  192.6 1.0 copy.31
  194.8 0.8 reshape.189
  195.6 1.3 dynamic-slice
  197.6 1.1 select_maximum_fusion
  199.6 1.3 convolution_add_fusion.6
  203.2 1.4 fusion.8
  205.5 1.2 fusion.48
  206.7 140.9 %all-reduce.3 = (f32[1,2432]{1,0:T(1,128)}, f32[1,2432]{1,0:T(1,128)}) all-reduce(f32[1,2432]{1,0:T(1,128)S(1)} %reduce_sum.76, f32[1,2432]{1,0:T(1,128)S(1)} %reduce_sum.78), channel_id=1, replica_groups=mesh['mem'=16,'sp'=32] {'sp'}, use_global_device_ids=true, to_apply=%region_8.9 | all-reduce | flops 4864 | bytes 38912 | tf_op jit(solution)/shard_map/psum | solution.py:85
  347.6 1.1 fusion.34
  348.7 148.1 %all-reduce.6.cloned.1.call-done = f32[2432,64]{0,1:T(8,128)} async-done(((f32[2432,64]{0,1:T(8,128)}), f32[2432,64]{0,1:T(8,128)}) %all-reduce.6.cloned.1.call-update) | async-done | bytes 622608
  496.7 0.9 constant_dynamic-slice_fusion
  497.6 64.3 %psum.21 = f32[76,64]{0,1:T(8,128)} all-reduce(f32[76,64]{0,1:T(8,128)S(1)} %constant_dynamic-slice_fusion), channel_id=1, replica_groups=mesh['mem'=16,'sp'=32] {'mem'}, use_global_device_ids=true, to_apply=%region_6.7 | all-reduce | flops 4864 | bytes 38912 | tf_op jit(solution)/shard_map/psum | solution.py:100
  (78 shorter events, 8.7 us)
Async XLA Ops:
  7.2 51.3 %copy-start = (bf16[1,8,128,512]{3,2,1,0:T(8,128)(2,1)S(1)}, bf16[1,8,128,512]{3,2,1,0:T(8,128)(2,1)}, u32[]{:S(2)}) copy-start(bf16[1,8,128,512]{3,2,1,0:T(8,128)(2,1)} %param.7) | copy-start | bytes 3145732
  7.2 53.9 %copy-start.13 = (bf16[3,3,16,16]{3,2,1,0:T(8,128)(2,1)S(1)}, bf16[3,3,16,16]{3,2,1,0:T(8,128)(2,1)}, u32[]{:S(2)}) copy-start(bf16[3,3,16,16]{3,2,1,0:T(8,128)(2,1)} %param.9) | copy-start | bytes 13828
  7.2 118.4 %all-gather.3.cloned.1.call-start = ((), (), s32[]{:S(2)}) async-start(), calls=%async_computation | async-start | bytes 4866048 | tf_op jit(solution)/shard_map/all_gather | solution.py:38
  56.3 64.3 %copy-start.1 = (bf16[1,64,2432]{2,1,0:T(8,128)(2,1)S(1)}, bf16[1,64,2432]{2,1,0:T(8,128)(2,1)}, u32[]{:S(2)}) copy-start(bf16[1,64,2432]{2,1,0:T(8,128)(2,1)} %param.10) | copy-start | bytes 933892
  58.4 438.4 %all-reduce.6.cloned.1.call-start = ((), (), s32[]{:S(2)}) async-start(), calls=%async_computation.1 | async-start | bytes 1245184
  58.5 65.4 %collective-permute-start = (bf16[1,1,128,512]{3,2,1,0:T(8,128)(2,1)S(1)}, bf16[1,1,128,512]{3,2,1,0:T(8,128)(2,1)S(1)}, u32[]{:S(2)}, u32[]{:S(2)}) collective-permute-start(bf16[1,1,128,512]{3,2,1,0:T(8,128)(2,1)S(1)} %get-tuple-element.19), channel_id=1, source_target_pairs={{0,1},{1,2},{2,3},{3,4},{4,5},{5,6},{6,7},{7,8},{8,9},{9,10},{10,1... | collective-permute-start | bytes 393224 | tf_op jit(solution)/shard_map/ppermute | solution.py:12
  59.8 64.1 %collective-permute-start.1 = (bf16[1,1,128,512]{3,2,1,0:T(8,128)(2,1)S(1)}, bf16[1,1,128,512]{3,2,1,0:T(8,128)(2,1)S(1)}, u32[]{:S(2)}, u32[]{:S(2)}) collective-permute-start(bf16[1,1,128,512]{3,2,1,0:T(8,128)(2,1)S(1)} %get-tuple-element.20), channel_id=1, source_target_pairs={{1,0},{2,1},{3,2},{4,3},{5,4},{6,5},{7,6},{8,7},{9,8},{10,9},{11,1... | collective-permute-start | bytes 393224 | tf_op jit(solution)/shard_map/ppermute | solution.py:15
  123.9 3.7 copy-start.11
  125.6 3.7 copy-start.2
  133.1 0.9 copy-start.12
  137.6 8.1 %copy-start.14 = (bf16[76,64]{0,1:T(8,128)(2,1)S(1)}, bf16[76,64]{0,1:T(8,128)(2,1)}, u32[]{:S(2)}) copy-start(bf16[76,64]{0,1:T(8,128)(2,1)} %param.13) | copy-start | bytes 29188
  137.6 56.1 %copy-start.10 = (bf16[1,1,16,512]{2,1,0,3:T(2,128)(2,1)S(1)}, bf16[1,1,16,512]{2,1,0,3:T(2,128)(2,1)}, u32[]{:S(2)}) copy-start(bf16[1,1,16,512]{2,1,0,3:T(2,128)(2,1)} %get-tuple-element.16) | copy-start | bytes 49156
  137.6 56.2 %copy-start.9 = (bf16[1,1,16,512]{2,1,0,3:T(2,128)(2,1)S(1)}, bf16[1,1,16,512]{2,1,0,3:T(2,128)(2,1)}, u32[]{:S(2)}) copy-start(bf16[1,1,16,512]{2,1,0,3:T(2,128)(2,1)} %get-tuple-element.15) | copy-start | bytes 49156
  137.6 56.3 %copy-start.8 = (bf16[1,1,16,512]{2,1,0,3:T(2,128)(2,1)S(1)}, bf16[1,1,16,512]{2,1,0,3:T(2,128)(2,1)}, u32[]{:S(2)}) copy-start(bf16[1,1,16,512]{2,1,0,3:T(2,128)(2,1)} %get-tuple-element.14) | copy-start | bytes 49156
  137.6 56.4 %copy-start.7 = (bf16[1,1,16,512]{2,1,0,3:T(2,128)(2,1)S(1)}, bf16[1,1,16,512]{2,1,0,3:T(2,128)(2,1)}, u32[]{:S(2)}) copy-start(bf16[1,1,16,512]{2,1,0,3:T(2,128)(2,1)} %get-tuple-element.13) | copy-start | bytes 49156
  137.6 56.5 %copy-start.6 = (bf16[1,1,16,512]{2,1,0,3:T(2,128)(2,1)S(1)}, bf16[1,1,16,512]{2,1,0,3:T(2,128)(2,1)}, u32[]{:S(2)}) copy-start(bf16[1,1,16,512]{2,1,0,3:T(2,128)(2,1)} %get-tuple-element.12) | copy-start | bytes 49156
  137.6 56.6 %copy-start.5 = (bf16[1,1,16,512]{2,1,0,3:T(2,128)(2,1)S(1)}, bf16[1,1,16,512]{2,1,0,3:T(2,128)(2,1)}, u32[]{:S(2)}) copy-start(bf16[1,1,16,512]{2,1,0,3:T(2,128)(2,1)} %get-tuple-element.11) | copy-start | bytes 49156
  140.8 53.4 %copy-start.4 = (bf16[1,1,16,512]{2,1,0,3:T(2,128)(2,1)S(1)}, bf16[1,1,16,512]{2,1,0,3:T(2,128)(2,1)}, u32[]{:S(2)}) copy-start(bf16[1,1,16,512]{2,1,0,3:T(2,128)(2,1)} %get-tuple-element.18) | copy-start | bytes 49156
  140.8 53.5 %copy-start.3 = (bf16[1,1,16,512]{2,1,0,3:T(2,128)(2,1)S(1)}, bf16[1,1,16,512]{2,1,0,3:T(2,128)(2,1)}, u32[]{:S(2)}) copy-start(bf16[1,1,16,512]{2,1,0,3:T(2,128)(2,1)} %get-tuple-element.10) | copy-start | bytes 49156
  141.6 56.1 %collective-permute-start.2 = (f32[1,1,64,512]{3,2,1,0:T(8,128)}, f32[1,1,64,512]{3,2,1,0:T(8,128)}, u32[]{:S(2)}, u32[]{:S(2)}) collective-permute-start(f32[1,1,64,512]{3,2,1,0:T(8,128)} %get-tuple-element.21), channel_id=1, source_target_pairs={{0,1},{1,2},{2,3},{3,4},{4,5},{5,6},{6,7},{7,8},{8,9},{9,10},{10,1... | collective-permute-start | bytes 393224 | tf_op jit(solution)/shard_map/ppermute | solution.py:12
  144.3 53.3 %collective-permute-start.3 = (f32[1,1,64,512]{3,2,1,0:T(8,128)}, f32[1,1,64,512]{3,2,1,0:T(8,128)}, u32[]{:S(2)}, u32[]{:S(2)}) collective-permute-start(f32[1,1,64,512]{3,2,1,0:T(8,128)} %get-tuple-element.22), channel_id=1, source_target_pairs={{1,0},{2,1},{3,2},{4,3},{5,4},{6,5},{7,6},{8,7},{9,8},{10,9},{11,1... | collective-permute-start | bytes 393224 | tf_op jit(solution)/shard_map/ppermute | solution.py:15
  193.6 2.0 copy-start.15
  193.6 4.0 copy-start.16
Sparse Core Ops, SparseCore 0:
  58.5 67.1 all-gather.2
  206.8 289.8 all-reduce.5
where the time goes:
time: 569 us
  blocking collectives  360 us (63%)
  waiting for transfers between devices  149 us (26%)
  matrix products  16.8 us (3%)
  between operations  15.1 us (3%)
  local copies, waits for them, and re-layouts  14.7 us (3%)
  starting transfers between devices  6.74 us (1%)
  other arithmetic  6.38 us (1%)
    unnamed x3, waiting for transfers between devices  148 us
    psum x1, blocking collectives, per_device(): lax.psum((jnp.sum(grad_mod, axis=1), jnp.sum(grad_mod * normed, axis=1)),...  141 us
    psum x1, blocking collectives, per_device(): grad_final = lax.psum(local_rows, 'mem')  64.3 us
    all_gather x1, blocking collectives, per_device(): lax.all_gather(input_weight, 'sp', axis=3, tiled=True)  59.4 us
    all_gather x1, blocking collectives, per_device(): partial_weight = lax.all_gather(conv_weight, 'mem', axis=3, tiled=True)  48.1 us
    all_gather x1, blocking collectives, per_device(): lax.all_gather(final_weight, 'sp', axis=0, tiled=True)  46.9 us
  transfers between devices with their start and end apart: 6, of which 2 were waited for; matrix products, arithmetic and copies ran while one was open for 2% of the time, Pallas kernels for 0%

commit v1 on v0

v1 whole, which is shorter than its diff:
```python
import jax
import jax.numpy as jnp
from jax import lax
from jax.experimental import pallas as pl
from jax.experimental.pallas import tpu as pltpu
from jax.sharding import PartitionSpec as P

MESH = pl.DeviceIdType.MESH
F32, BF16 = jnp.float32, jnp.bfloat16
OWNERS = (0, 2, 5, 12, 15)


def iota(shape, dim):
    return lax.broadcasted_iota(jnp.int32, shape, dim)


def kernel(
    g_hbm, cw_ref, iw_ref, hid_hbm, shift_ref, scale_ref, wf_ref,
    gh_ref, gf_ref, gs_ref, gsh_ref,
    gall, hall, kp0, kp1, rsb0, rsb1, kb0, kb1, sx, ps, rhs, zacc, lat, tp, tpr, halo,
    wfb, wff, nrm, inv, ntf, nt2, gtd, nch, nrb, gsp, gsb, cm, mrb, mab,
    ssem, lsem, rs0, rs1, rz0, rz1, ry0, ry1, rx0, rx1, rg, rh, rwy, rwx, rwc, rt, rup, rdn, rn, rgs, rm1, rm2,
):
    mem, sp = lax.axis_index("mem"), lax.axis_index("sp")
    ylo, z = mem // 8, mem % 8
    core, j = sp % 2, sp // 2
    yhi, x = j // 4, j % 4
    other = 1 - core
    pending = []

    def send(src, dst, recv, device, cond=None):
        copy = pltpu.make_async_remote_copy(
            src_ref=src, dst_ref=dst, send_sem=ssem.at[len(pending)], recv_sem=recv,
            device_id=device, device_id_type=MESH,
        )
        pending.append((copy, cond))
        if cond is None:
            copy.start()
        else:
            pl.when(cond)(copy.start)

    def arrived(ref, sem):
        pltpu.make_async_copy(ref, ref, sem).wait()

    barrier = pltpu.get_barrier_semaphore()

    def greet_sp(step, carry):
        pl.semaphore_signal(barrier, inc=1, device_id=(mem, (sp + step) % 32), device_id_type=MESH)
        return carry

    def greet_mem(step, carry):
        pl.semaphore_signal(barrier, inc=1, device_id=((mem + step) % 16, sp), device_id_type=MESH)
        return carry

    def greet_cross(step, carry):
        there = (((yhi + step) % 4) * 4 + x) * 2 + core
        pl.semaphore_signal(barrier, inc=1, device_id=((1 - ylo) * 8 + z, there), device_id_type=MESH)
        return carry

    lax.fori_loop(1, 32, greet_sp, 0)
    lax.fori_loop(1, 16, greet_mem, 0)
    lax.fori_loop(1, 4, greet_cross, 0)

    own_g = pltpu.make_async_copy(
        g_hbm.at[0, :, :, pl.ds(pl.multiple_of(core * 256, 256), 256)],
        gall.at[pl.ds(core * 8, 8)], lsem.at[0])
    own_g.start()
    own_h = pltpu.make_async_copy(hid_hbm.at[0], hall.at[core], lsem.at[1])
    own_h.start()

    iw = iw_ref[...]
    both = jnp.concatenate([iw[:128]] + [iw[128:144]] * 8, axis=0)
    cw = jnp.concatenate([cw_ref[k] for k in range(9)], axis=1)
    part = lax.dot_general(cw, both, (((0,), (1,)), ((), ())), preferred_element_type=F32)
    part = part.reshape(18, 16, 256)
    lane16 = iota((16, 128), 1) // 16
    tiles = [part[k, :, :128] for k in range(18)]
    for first in range(0, 24, 8):
        packed = jnp.zeros((16, 128), F32)
        for k in range(first, min(first + 8, 18)):
            packed = jnp.where(lane16 == k - first, part[k, :, 128:], packed)
        tiles.append(packed)
    for t in range(16):
        kp0[t] = tiles[t].astype(BF16)
    for t in range(8):
        kp1[t] = (tiles[16 + t] if t < 5 else jnp.zeros((16, 128), F32)).astype(BF16)

    wf = wf_ref[...].astype(F32)
    wide = jnp.concatenate([wf[:38], wf[38:76]], axis=1)
    wide = jnp.concatenate([wide, jnp.zeros((10, 128), F32)], axis=0)
    wfb[core, yhi, x] = wide.astype(BF16)

    pl.semaphore_wait(barrier, 49)

    for step in range(16):
        there = (j + step) % 16
        target = (mem, there * 2 + ylo)
        if step:
            send(kp0.at[there], rsb0.at[sp], rs0, target)
        else:
            send(kp0.at[there], rsb0.at[sp], rs0, target, core != ylo)

            @pl.when(core == ylo)
            def _():
                pltpu.make_async_copy(kp0.at[j], rsb0.at[sp], rs0).start()

    for step in range(8):
        there = (j + step) % 8
        target = (mem, there * 2 + ylo)
        if step:
            send(kp1.at[there], rsb1.at[sp], rs1, target)
        else:
            mine = jnp.logical_and(core == ylo, j < 8)
            send(kp1.at[there], rsb1.at[sp], rs1, target, jnp.logical_not(mine))

            @pl.when(mine)
            def _():
                pltpu.make_async_copy(kp1.at[j], rsb1.at[sp], rs1).start()

    partner = (mem, j * 2 + other)
    send(g_hbm.at[0, :, :, pl.ds(pl.multiple_of(other * 256, 256), 256)], gall.at[pl.ds(core * 8, 8)], rg, partner)
    send(hid_hbm.at[0], hall.at[core], rh, partner)
    for step in range(1, 4):
        send(wfb.at[core, yhi, x], wfb.at[core, yhi, x], rwy.at[yhi], (mem, (((yhi + step) % 4) * 4 + x) * 2 + core))

    lanes = iota((48, 2432), 1)
    rows = iota((48, 2432), 0)
    hit_a, hit_b = lanes == sp * 76 + rows, lanes == sp * 76 + 38 + rows
    left = iota((48, 128), 1) < 64
    scale, shift = scale_ref[...], shift_ref[...]

    def pick(values):
        a = jnp.sum(jnp.where(hit_a, values, 0.0), axis=1, keepdims=True)
        b = jnp.sum(jnp.where(hit_b, values, 0.0), axis=1, keepdims=True)
        return jnp.where(left, a, b)

    own_scale, own_shift = 1.0 + pick(scale), pick(shift)

    source = core == ylo
    first_half = yhi < 2
    both_slots = jnp.logical_and(source, first_half)

    @pl.when(source)
    def _():
        arrived(rsb0, rs0)
        kb0[j, z] = jnp.sum(rsb0[...].astype(F32), axis=0).astype(BF16)

    @pl.when(both_slots)
    def _():
        arrived(rsb1, rs1)
        kb1[j, z] = jnp.sum(rsb1[...].astype(F32), axis=0).astype(BF16)

    for step in range(1, 8):
        target = (ylo * 8 + (z + step) % 8, sp)
        send(kb0.at[j, z], kb0.at[j, z], rz0, target, source)
        send(kb1.at[j % 8, z], kb1.at[j % 8, z], rz1, target, both_slots)

    @pl.when(source)
    def _():
        arrived(kb0.at[0, pl.ds(0, 7)], rz0)

    @pl.when(both_slots)
    def _():
        arrived(kb1.at[0, pl.ds(0, 7)], rz1)

    for dlo in range(2):
        for step in range(4):
            if dlo + step == 0:
                continue
            there = (((yhi + step) % 4) * 4 + x) * 2 + core
            target = (((ylo + dlo) % 2) * 8 + z, there)
            send(kb0.at[j], kb0.at[j], ry0.at[yhi], target, source)
            send(kb1.at[j % 8], kb1.at[j % 8], ry1.at[yhi % 2], target, both_slots)

    for piece in range(4):
        missing = jnp.logical_not(jnp.logical_and(source, yhi == piece))
        here = piece * 4 + x

        @pl.when(missing)
        def _():
            arrived(kb0.at[here], ry0.at[piece])
            if piece < 2:
                arrived(kb1.at[here], ry1.at[piece])

        for step in range(1, 4):
            target = (mem, (yhi * 4 + (x + step) % 4) * 2 + core)
            send(kb0.at[here], kb0.at[here], rx0, target)
            if piece < 2:
                send(kb1.at[here], kb1.at[here], rx1, target)

    for piece in range(4):
        @pl.when(yhi != piece)
        def _():
            arrived(wfb.at[core, piece, x], rwy.at[piece])
    for step in range(1, 4):
        send(wfb.at[core, :, x], wfb.at[core, :, x], rwx.at[x], (mem, (yhi * 4 + (x + step) % 4) * 2 + core))

    own_g.wait()
    arrived(gall.at[pl.ds(0, 8)], rg)
    sx[pl.ds(0, 64), pl.ds(768, 1536)] = jnp.zeros((64, 1536), BF16)
    sx[pl.ds(576, 64), pl.ds(0, 1536)] = jnp.zeros((64, 1536), BF16)
    for half in range(2):
        ps[half, pl.ds(0, 8), :] = jnp.zeros((8, 128), F32)
        ps[half, pl.ds(136, 8), :] = jnp.zeros((8, 128), F32)

    def columns(start):
        return jnp.concatenate([ps.at[half][pl.ds(start, 64, stride=2), :] for half in range(2)], axis=1)

    for r in range(-1, 16):
        if r == -1:
            pair = gall[0].astype(F32)
        elif r == 15:
            pair = gall[15].astype(F32)
        else:
            pair = gall[r].astype(F32) + gall[r + 1].astype(F32)
        for half in range(2):
            ps[half, pl.ds(8, 128), :] = pair[:, 128 * half : 128 * half + 128]
        before, even, odd, after = columns(7), columns(8), columns(9), columns(10)
        sums = jnp.concatenate([odd + after, even + odd, before + even], axis=1)
        if r % 2 == 0:
            places = ((r // 2, 1),)
        else:
            places = (((r - 1) // 2, 0), ((r + 1) // 2, 2))
        for i, a in places:
            kept = sums
            if i == -1:
                kept = jnp.where(j > 0, sums, 0.0)
            if i == 8:
                kept = jnp.where(j < 15, sums, 0.0)
            sx[pl.ds((i + 1) * 64, 64), pl.ds(a * 768, 768)] = kept.astype(BF16)

    own_h.wait()
    arrived(hall.at[0], rh)
    for k in range(2):
        values = hall[k].astype(F32)
        centred = values - jnp.mean(values, axis=-1, keepdims=True)
        inverse = lax.rsqrt(jnp.mean(centred * centred, axis=-1, keepdims=True) + 1e-06)
        nrm[pl.ds(k * 64, 64), :] = centred * inverse
        inv[pl.ds(k * 64, 64), :] = jnp.broadcast_to(inverse, (64, 128))
    for k in range(19):
        ntf[pl.ds(k * 128, 128), :] = nrm[:, pl.ds(k * 128, 128)].T
    ntf[pl.ds(2432, 16), :] = jnp.zeros((16, 128), F32)
    row = iota((48, 128), 0)
    for k in range(16):
        for h in range(2):
            a = ntf[pl.ds(152 * k + 38 * h, 48), :]
            b = ntf[pl.ds(152 * k + 76 + 38 * h, 48), :]
            v = jnp.where(core == 0, a, b)
            v = jnp.where(row < 38, v, jnp.where(row == 38, 1.0, 0.0))
            nt2[pl.ds((2 * k + h) * 48, 48), :] = v.astype(BF16)

    for piece in range(4):
        @pl.when(x != piece)
        def _():
            arrived(wfb.at[core, :, piece], rwx.at[piece])
    send(wfb.at[core], wfb.at[core], rwc, partner)

    arrived(kb0.at[pl.ds(0, 12)], rx0)
    arrived(kb1.at[pl.ds(0, 6)], rx1)

    def tile(t):
        return kb0[t] if t < 16 else kb1[t - 16]

    group = iota((8, 16, 128), 2) // 16
    for k in range(9):
        main, last = [], []
        for h in range(2):
            t = 2 * k + h
            main.append(tile(t))
            packed = tile(18 + t // 8)
            last.append(jnp.where(group == t % 8, packed, jnp.zeros_like(packed)))
        pieces = []
        for zz in range(8):
            for h in range(2):
                pieces.append(jnp.concatenate([main[h][zz], last[h][zz]], axis=1))
        rhs[pl.ds(k * 256, 256), :] = jnp.concatenate(pieces, axis=0)

    zacc[...] = jnp.dot(sx[...], rhs[...], preferred_element_type=F32)

    field, corner = zacc[:, :128], zacc[:, 128:]
    column = iota((640, 128), 0) % 64
    g8 = iota((640, 128), 1) // 16
    tap_r, tap_c = g8 // 3, g8 % 3
    minus = jnp.where(column == 63, 0.0, pltpu.roll(field, 639, axis=0))
    plus = jnp.where(column == 0, 0.0, pltpu.roll(field, 1, axis=0))
    corner = jnp.where(column == 0, 0.0, pltpu.roll(corner, 1, axis=0))
    moved = jnp.where(tap_c == 0, minus, jnp.where(tap_c == 1, field, plus))
    none = jnp.zeros((64, 128), F32)
    total = jnp.concatenate([jnp.where(tap_r == 0, moved, 0.0), none, none], axis=0)
    total += jnp.concatenate([none, jnp.where(tap_r == 1, moved, 0.0), none], axis=0)
    total += jnp.concatenate([none, none, jnp.where(tap_r == 2, moved, 0.0) + corner], axis=0)
    total += pltpu.roll(total, 64, axis=1)
    total += pltpu.roll(total, 32, axis=1)
    total += pltpu.roll(total, 16, axis=1)
    lat[...] = total * (1.0 / 1.5305)
    g4 = (iota((32, 128), 1) // 16) % 4
    for r in range(6):
        value = jnp.zeros((32, 128), F32)
        for p in range(2):
            for s in range(2):
                value = jnp.where(g4 == 2 * p + s, lat[pl.ds((2 * r + p) * 64 + s, 32, stride=2), :], value)
        tp[r] = value

    send(tp.at[pl.ds(1, 4)], tpr, rt, partner)
    for c in range(2):
        send(tp.at[0], halo.at[1, core], rdn, (mem, jnp.maximum(2 * j - 2 + c, 0)), j > 0)
        send(tp.at[5], halo.at[0, core], rup, (mem, jnp.minimum(2 * j + 2 + c, 31)), j < 15)

    @pl.when(j == 0)
    def _():
        halo[0] = jnp.zeros((2, 32, 128), F32)

    @pl.when(j == 15)
    def _():
        halo[1] = jnp.zeros((2, 32, 128), F32)

    arrived(wfb.at[0], rwc)
    left = iota((48, 128), 1) < 64
    for k in range(16):
        for c in range(2):
            block = wfb[c, k // 4, k % 4].astype(F32)
            at = 76 * (2 * k + c)
            wff[pl.ds(at, 40), :] = jnp.where(left, block, 0.0)[:40]
            wff[pl.ds(at + 38, 40), :] = jnp.where(left, pltpu.roll(block, 64, axis=1), 0.0)[:40]
    whole = wff[pl.ds(0, 2432), :].astype(BF16)

    arrived(tpr, rt)

    @pl.when(j > 0)
    def _():
        arrived(halo.at[0], rup)

    @pl.when(j < 15)
    def _():
        arrived(halo.at[1], rdn)

    for r in range(4):
        value = tp[r + 1] + tpr[r]
        if r == 0:
            value += halo[0, 0] + halo[0, 1]
        if r == 3:
            value += halo[1, 0] + halo[1, 1]
        gtd[pl.ds(r * 32, 32), :] = value.astype(BF16)

    prod = jnp.dot(nt2[...], gtd[...], preferred_element_type=F32).reshape(32, 48, 128)
    for k in range(16):
        nch[k] = jnp.where(left, prod[2 * k], prod[2 * k + 1]).astype(BF16)
    for step in range(1, 16):
        there = (j + step) % 16
        send(nch.at[there], nrb.at[j], rn, (mem, there * 2 + core))
    nrb[j] = nch[j]

    own_rows = pl.ds(pl.multiple_of(core * 64, 64), 64)
    gmod = lax.dot_general(gtd[own_rows, :], whole, (((1,), (1,)), ((), ())), preferred_element_type=F32)
    normed = nrm[own_rows, :]
    dn = gmod * (1.0 + scale)
    m1 = jnp.mean(dn, axis=-1, keepdims=True)
    m2 = jnp.mean(dn * normed, axis=-1, keepdims=True)
    gh_ref[0] = ((dn - m1 - normed * m2) * inv[own_rows, 0:1]).astype(BF16)

    arrived(nrb.at[pl.ds(0, 15)], rn)
    member = jnp.sum(nrb[...].astype(F32), axis=0)

    tokens_sum = member[38:39, :]
    weighted = own_scale * member + own_shift * tokens_sum
    for t in range(5):
        cm[t] = weighted[8 * t : 8 * t + 8]
        target = (OWNERS[t], sp)
        send(cm.at[t], mrb.at[mem], rm1, target, mem != OWNERS[t])

        @pl.when(mem == OWNERS[t])
        def _():
            mrb[mem] = cm[t]

    scaled = member * wide
    square = jnp.concatenate([scaled, jnp.zeros((80, 128), F32)], axis=0).T
    a = jnp.sum(square[:64], axis=0, keepdims=True)
    b = jnp.sum(square[64:], axis=0, keepdims=True)
    gsp[...] = jnp.concatenate([a, b, jnp.zeros((6, 128), F32)], axis=0)
    for step in range(1, 32):
        send(gsp, gsb.at[sp], rgs, (mem, (sp + step) % 32))
    gsb[sp] = gsp[...]

    high = tokens_sum.astype(BF16)
    low = (tokens_sum - high.astype(F32)).astype(BF16)
    pair = jnp.concatenate([high, low, jnp.zeros((14, 128), BF16)], axis=0)
    sums = lax.dot_general(pair, whole, (((1,), (1,)), ((), ())), preferred_element_type=F32)
    gsh_ref[...] = sums[0:1] + sums[1:2]

    for t in range(5):
        @pl.when(mem == OWNERS[t])
        def _():
            arrived(mrb.at[pl.ds(0, 15)], rm1)
            mab[t] = jnp.sum(mrb[...], axis=0)

        for step in range(1, 16):
            send(mab.at[t], mab.at[t], rm2.at[t], ((OWNERS[t] + step) % 16, sp), mem == OWNERS[t])

    arrived(gsb.at[pl.ds(0, 31)], rgs)
    for s in range(32):
        for h in range(2):
            gs_ref[:, pl.ds(76 * s + 38 * h, 38)] = gsb[s, h : h + 1, 0:38]

    for t in range(5):
        @pl.when(mem != OWNERS[t])
        def _():
            arrived(mab.at[t], rm2.at[t])
    final = mab[...].reshape(40, 128)
    gf_ref[pl.ds(0, 38), :] = final[:38, :64]
    gf_ref[pl.ds(38, 38), :] = final[:38, 64:]

    for copy, cond in pending:
        if cond is None:
            copy.wait_send()
        else:
            pl.when(cond)(copy.wait_send)


def per_device(grad_image, conv_weight, input_weight, hidden, shift, scale, final_weight):
    vmem = pl.BlockSpec(memory_space=pltpu.VMEM)
    hbm = pl.BlockSpec(memory_space=pl.ANY)
    dma = pltpu.SemaphoreType.DMA
    return pl.pallas_call(
        kernel,
        out_shape=(
            jax.ShapeDtypeStruct((1, 64, 2432), BF16),
            jax.ShapeDtypeStruct((76, 64), F32),
            jax.ShapeDtypeStruct((1, 2432), F32),
            jax.ShapeDtypeStruct((1, 2432), F32),
        ),
        in_specs=[hbm, vmem, vmem, hbm, vmem, vmem, vmem],
        out_specs=(vmem,) * 4,
        scratch_shapes=[
            pltpu.VMEM((16, 128, 256), BF16),
            pltpu.VMEM((2, 64, 2432), BF16),
            pltpu.VMEM((16, 16, 128), BF16),
            pltpu.VMEM((8, 16, 128), BF16),
            pltpu.VMEM((32, 16, 128), BF16),
            pltpu.VMEM((32, 16, 128), BF16),
            pltpu.VMEM((16, 8, 16, 128), BF16),
            pltpu.VMEM((8, 8, 16, 128), BF16),
            pltpu.VMEM((640, 2304), BF16),
            pltpu.VMEM((2, 144, 128), F32),
            pltpu.VMEM((2304, 256), BF16),
            pltpu.VMEM((640, 256), F32),
            pltpu.VMEM((768, 128), F32),
            pltpu.VMEM((6, 32, 128), F32),
            pltpu.VMEM((4, 32, 128), F32),
            pltpu.VMEM((2, 2, 32, 128), F32),
            pltpu.VMEM((2, 4, 4, 48, 128), BF16),
            pltpu.VMEM((2440, 128), F32),
            pltpu.VMEM((128, 2432), F32),
            pltpu.VMEM((128, 128), F32),
            pltpu.VMEM((2448, 128), F32),
            pltpu.VMEM((1536, 128), BF16),
            pltpu.VMEM((128, 128), BF16),
            pltpu.VMEM((16, 48, 128), BF16),
            pltpu.VMEM((16, 48, 128), BF16),
            pltpu.VMEM((8, 128), F32),
            pltpu.VMEM((32, 8, 128), F32),
            pltpu.VMEM((5, 8, 128), F32),
            pltpu.VMEM((16, 8, 128), F32),
            pltpu.VMEM((5, 8, 128), F32),
            dma((220,)),
            dma((2,)),
            dma, dma,
            dma, dma,
            dma((4,)), dma((2,)),
            dma, dma,
            dma, dma,
            dma((4,)), dma((4,)), dma,
            dma, dma, dma,
            dma, dma, dma, dma((5,)),
        ],
        compiler_params=pltpu.CompilerParams(
            collective_id=0, has_side_effects=True, vmem_limit_bytes=48 * 1024 * 1024
        ),
        cost_estimate=pl.CostEstimate(flops=1_000_000_000, bytes_accessed=2_000_000, transcendentals=0),
    )(
        grad_image,
        conv_weight.reshape(9, 16, 32),
        input_weight.reshape(144, 16),
        hidden,
        shift,
        scale,
        final_weight,
    )


def solution(mesh):
    placed = (
        P("mem", "sp", None, None),
        P(None, None, "sp", "mem"),
        P(None, None, None, "sp"),
        P("mem", "sp", None),
        P("mem", None),
        P("mem", None),
        P("sp", None),
    )
    return jax.shard_map(
        per_device,
        mesh=mesh,
        in_specs=placed,
        out_specs=(P("mem", "sp", None), P("sp", None), P("mem", None), P("mem", None)),
        check_vma=False,
    )
```

time: 569 us -> 81.5 us (0.14)
  the two profiles are of different devices: /device:TPU:8 before, /device:TPU:6 now
where the time goes in v1:
time: 81.5 us; the launch traced here: 80.6 us
  Pallas kernels  72.1 us (88%)
  local copies, waits for them, and re-layouts  7.8 us (10%)
    pallas_call x1, Pallas kernels, per_device(): pl.pallas_call(kernel, out_shape=(jax.ShapeDtypeStruct((1, 64, 2432), BF1...  72.1 us
    unnamed x16, local copies, waits for them, and re-layouts  7.1 us

profile of v1, /device:TPU:6, one launch (start us, length us, event | category | flops | bytes accessed | tf_op | source)
XLA Modules:
  0.0 80.6 jit_solution(17879656408137343708)
XLA Ops:
  0.6 0.0 copy-start.2
  0.6 0.8 %copy.11.wf_ref = bf16[76,64]{1,0:T(8,128)(2,1)S(1)} copy(bf16[76,64]{0,1:T(8,128)(2,1)} %param.13) | data formatting | bytes 19456 | tf_op args[6]
  1.5 0.0 copy-done.2
  1.5 0.0 copy-start
  1.5 1.2 %copy-done = bf16[1,8,128,512]{3,2,1,0:T(8,128)(2,1)S(1)} copy-done((bf16[1,8,128,512]{3,2,1,0:T(8,128)(2,1)S(1)}, bf16[1,8,128,512]{3,2,1,0:T(8,128)(2,1)}, u32[]{:S(2)}) %copy-start) | copy-done | bytes 1048600
  2.7 0.0 copy-start.1
  2.7 1.0 %copy-done.1 = bf16[1,64,2432]{2,1,0:T(8,128)(2,1)S(1)} copy-done((bf16[1,64,2432]{2,1,0:T(8,128)(2,1)S(1)}, bf16[1,64,2432]{2,1,0:T(8,128)(2,1)}, u32[]{:S(2)}) %copy-start.1) | copy-done | bytes 311320
  3.7 0.0 copy-start.3
  3.7 0.8 copy-done.3
  4.4 0.0 copy-start.4
  4.4 0.7 copy-done.4
  5.1 0.0 copy-start.5
  5.1 0.7 copy-done.5
  5.8 72.1 %shard_map.102 = (bf16[1,64,2432]{2,1,0:T(8,128)(2,1)S(1)}, f32[76,64]{1,0:T(8,128)S(1)}, f32[1,2432]{1,0:T(1,128)S(1)}, f32[1,2432]{1,0:T(1,128)S(1)}) custom-call(bf16[1,8,128,512]{3,2,1,0:T(8,128)(2,1)S(1)} %copy-done, bf16[9,16,32]{2,1,0:T(8,128)(2,1)S(1)} %bitcast.2, bf16[144,16]{1,0:T(8,128)(2,1)S(1)} %bitcast.3, bf16[1,64,2432]{2,1,0:T(8,128)(2,1)S(1)} %copy-done.1, ...), custom_call_target="tpu_custom_call" | custom-call | flops 1000000000 | bytes 2000000 | tf_op jit(solution)/shard_map/pallas_call | solution.py:423
  78.0 0.7 copy.12
  78.7 0.7 copy.16
  79.4 0.6 copy.17
  80.0 0.6 copy.18
Async XLA Ops:
  0.6 0.8 %copy-start.2 = (bf16[3,3,16,32]{3,2,1,0:T(8,128)(2,1)S(1)}, bf16[3,3,16,32]{3,2,1,0:T(8,128)(2,1)}, u32[]{:S(2)}) copy-start(bf16[3,3,16,32]{3,2,1,0:T(8,128)(2,1)} %param.8) | copy-start | bytes 27652
  1.5 1.2 %copy-start = (bf16[1,8,128,512]{3,2,1,0:T(8,128)(2,1)S(1)}, bf16[1,8,128,512]{3,2,1,0:T(8,128)(2,1)}, u32[]{:S(2)}) copy-start(bf16[1,8,128,512]{3,2,1,0:T(8,128)(2,1)} %g_hbm.1) | copy-start | bytes 3145732
  2.7 1.0 %copy-start.1 = (bf16[1,64,2432]{2,1,0:T(8,128)(2,1)S(1)}, bf16[1,64,2432]{2,1,0:T(8,128)(2,1)}, u32[]{:S(2)}) copy-start(bf16[1,64,2432]{2,1,0:T(8,128)(2,1)} %hid_hbm.1) | copy-start | bytes 933892
  3.7 0.8 copy-start.3
  4.4 0.7 copy-start.4
  5.1 0.7 copy-start.5

commit v2 on v1

v2 whole, which is shorter than its diff:
```python
import jax
import jax.numpy as jnp
from jax import lax
from jax.experimental import pallas as pl
from jax.experimental.pallas import tpu as pltpu
from jax.sharding import PartitionSpec as P

MESH = pl.DeviceIdType.MESH
F32, BF16 = jnp.float32, jnp.bfloat16
SPLIT = 10


def iota(shape, dim):
    return lax.broadcasted_iota(jnp.int32, shape, dim)


def kernel(
    g_hbm, cw_hbm, iw_hbm, hid_hbm, shift_hbm, scale_hbm, wf_hbm,
    gh_ref, gf_ref, gs_ref, gsh_ref,
    cwv, iwv, shv, scv, wfv,
    gall, hall, gother, pk, raw, kb, sx, ps, rhs, zacc, lat, tp, tpr, edge, halo,
    wfb, wff, whole, nrm, inv, ntf, nt2, gtd, nch, nrb, gmod, ghv, gst, cmb, mrb,
    ssem, lsem, rraw, rz, rzb, ry, ryb, rg, rh, rhu, rhd, rwy, rwx, rwc, rt, rn, rgc, rm,
):
    mem, sp = lax.axis_index("mem"), lax.axis_index("sp")
    ylo, z = mem // 8, mem % 8
    core, j = sp % 2, sp // 2
    yhi, x = j // 4, j % 4
    other = 1 - core
    pending = []
    used = [0]

    def send(src, dst, recv, device, cond=None):
        copy = pltpu.make_async_remote_copy(
            src_ref=src, dst_ref=dst, send_sem=ssem.at[used[0]], recv_sem=recv,
            device_id=device, device_id_type=MESH,
        )
        used[0] += 1
        pending.append((copy, cond))
        if cond is None:
            copy.start()
        else:
            pl.when(cond)(copy.start)

    def flush():
        for copy, cond in pending:
            if cond is None:
                copy.wait_send()
            else:
                pl.when(cond)(copy.wait_send)
        pending.clear()

    def arrived(ref, sem):
        pltpu.make_async_copy(ref, ref, sem).wait()

    barrier = pltpu.get_barrier_semaphore()

    def greet(device, cond=None):
        def signal():
            pl.semaphore_signal(barrier, inc=1, device_id=device, device_id_type=MESH)

        if cond is None:
            signal()
        else:
            pl.when(cond)(signal)

    def greet_sp(step, carry):
        greet((mem, (sp + step) % 32))
        return carry

    def greet_mem(step, carry):
        greet(((mem + step) % 16, sp))
        return carry

    lax.fori_loop(1, 32, greet_sp, 0)
    lax.fori_loop(1, 16, greet_mem, 0)

    loads = [
        (cw_hbm, cwv), (iw_hbm, iwv), (wf_hbm, wfv), (shift_hbm, shv), (scale_hbm, scv),
        (g_hbm.at[0, :, :, pl.ds(pl.multiple_of(core * 256, 256), 256)], gall.at[pl.ds(core * 8, 8)]),
        (hid_hbm.at[0], hall.at[core]),
        (g_hbm.at[0, :, :, pl.ds(pl.multiple_of(other * 256, 256), 256)], gother),
    ]
    loads = [pltpu.make_async_copy(src, dst, lsem.at[k]) for k, (src, dst) in enumerate(loads)]
    for copy in loads:
        copy.start()

    loads[0].wait()
    loads[1].wait()
    taps = iwv[...].astype(F32).T.astype(BF16)
    pk[...] = jnp.concatenate(
        [taps[:, :128]] + [cwv[k] for k in range(9)] + [taps[:, 128:], jnp.zeros((16, 80), BF16)], axis=1)

    loads[2].wait()
    wf = jnp.concatenate([wfv[...].astype(F32), jnp.zeros((64, 52), F32)], axis=1).T
    wide = jnp.concatenate([wf[:38], wf[38:76]], axis=1)
    wide = jnp.concatenate([wide, jnp.zeros((10, 128), F32)], axis=0)
    wfb[core, yhi, x] = wide.astype(BF16)

    pl.semaphore_wait(barrier, 46)

    source = core == ylo
    for step in range(16):
        target = (mem, ((j + step) % 16) * 2 + ylo)
        if step:
            send(pk, raw.at[sp], rraw, target)
        else:
            send(pk, raw.at[sp], rraw, target, jnp.logical_not(source))

    @pl.when(source)
    def _():
        pltpu.make_async_copy(pk, raw.at[sp], rraw).start()

    for step in range(1, 4):
        send(wfb.at[core, yhi, x], wfb.at[core, yhi, x], rwy.at[yhi], (mem, (((yhi + step) % 4) * 4 + x) * 2 + core))

    partner = (mem, j * 2 + other)
    loads[6].wait()
    send(hall.at[core], hall.at[core], rh, partner)
    loads[7].wait()
    send(gother, gall.at[pl.ds(core * 8, 8)], rg, partner)

    loads[3].wait()
    loads[4].wait()
    lanes = iota((48, 2432), 1)
    rows = iota((48, 2432), 0)
    hit_a, hit_b = lanes == sp * 76 + rows, lanes == sp * 76 + 38 + rows
    left = iota((48, 128), 1) < 64
    scale, shift = scv[...], shv[...]

    def pick(values):
        a = jnp.sum(jnp.where(hit_a, values, 0.0), axis=1, keepdims=True)
        b = jnp.sum(jnp.where(hit_b, values, 0.0), axis=1, keepdims=True)
        return jnp.where(left, a, b)

    own_scale, own_shift = 1.0 + pick(scale), pick(shift)

    arrived(hall.at[0], rh)
    for k in range(2):
        values = hall[k].astype(F32)
        centred = values - jnp.mean(values, axis=-1, keepdims=True)
        inverse = lax.rsqrt(jnp.mean(centred * centred, axis=-1, keepdims=True) + 1e-06)
        nrm[pl.ds(k * 64, 64), :] = centred * inverse
        inv[pl.ds(k * 64, 64), :] = jnp.broadcast_to(inverse, (64, 128))
    for k in range(19):
        ntf[pl.ds(k * 128, 128), :] = nrm[:, pl.ds(k * 128, 128)].T
    ntf[pl.ds(2432, 16), :] = jnp.zeros((16, 128), F32)
    row = iota((48, 128), 0)
    for k in range(16):
        for h in range(2):
            a = ntf[pl.ds(152 * k + 38 * h, 48), :]
            b = ntf[pl.ds(152 * k + 76 + 38 * h, 48), :]
            v = jnp.where(core == 0, a, b)
            v = jnp.where(row < 38, v, jnp.where(row == 38, 1.0, 0.0))
            nt2[pl.ds((2 * k + h) * 48, 48), :] = v.astype(BF16)

    loads[5].wait()
    arrived(gall.at[pl.ds(0, 8)], rg)

    for half in range(2):
        ps[half, pl.ds(0, 8), :] = jnp.zeros((8, 128), F32)
        ps[half, pl.ds(136, 8), :] = jnp.zeros((8, 128), F32)

    def columns(start):
        return jnp.concatenate([ps.at[half][pl.ds(start, 64, stride=2), :] for half in range(2)], axis=1)

    sx[pl.ds(0, 64), pl.ds(768, 1536)] = jnp.zeros((64, 1536), BF16)
    sx[pl.ds(576, 64), pl.ds(0, 1536)] = jnp.zeros((64, 1536), BF16)
    for r in range(-1, 16):
        pair = gall[max(r, 0)].astype(F32)
        if 0 <= r < 15:
            pair += gall[r + 1].astype(F32)
        for half in range(2):
            ps[half, pl.ds(8, 128), :] = pair[:, 128 * half : 128 * half + 128]
        before, even, odd, after = columns(7), columns(8), columns(9), columns(10)
        sums = jnp.concatenate([odd + after, even + odd, before + even], axis=1)
        if r % 2 == 0:
            places = ((r // 2, 1),)
        else:
            places = (((r - 1) // 2, 0), ((r + 1) // 2, 2))
        for i, a in places:
            kept = sums
            if i == -1:
                kept = jnp.where(j > 0, sums, 0.0)
            if i == 8:
                kept = jnp.where(j < 15, sums, 0.0)
            sx[pl.ds((i + 1) * 64, 64), pl.ds(a * 768, 768)] = kept.astype(BF16)

    for piece in range(4):
        @pl.when(yhi != piece)
        def _():
            arrived(wfb.at[core, piece, x], rwy.at[piece])
    for step in range(1, 4):
        send(wfb.at[core, :, x], wfb.at[core, :, x], rwx.at[x], (mem, (yhi * 4 + (x + step) % 4) * 2 + core))

    lane16 = iota((16, 128), 1) // 16

    @pl.when(source)
    def _():
        arrived(raw, rraw)
        every = raw[...].reshape(512, 512)
        ends = jnp.concatenate([every[:, :128], every[:, 384:]], axis=1)
        part = lax.dot_general(every[:, 128:], ends, (((0,), (0,)), ((), ())), preferred_element_type=F32)
        for k in range(18):
            kb[z, k] = part[16 * k : 16 * k + 16, :128].astype(BF16)
        for first in range(0, 24, 8):
            packed = jnp.zeros((16, 128), F32)
            for k in range(first, min(first + 8, 18)):
                moved = pltpu.roll(part[16 * k : 16 * k + 16, 128:], (16 * (k - first) - 32) % 128, axis=1)
                packed = jnp.where(lane16 == k - first, moved, packed)
            kb[z, 18 + first // 8] = packed.astype(BF16)

    across = ((1 - ylo) * 8 + z, sp)
    order = (1, 7, 2, 6, 3, 5, 4)
    sink = jnp.logical_not(source)
    one, two = pl.ds(0, SPLIT), pl.ds(SPLIT, 21 - SPLIT)

    send(kb.at[z, two], kb.at[z, two], ryb, across, source)
    for d in order:
        send(kb.at[z, one], kb.at[z, one], rz.at[z], (ylo * 8 + (z + d) % 8, sp), source)
    send(kb.at[z, one], kb.at[z, one], ry, across, source)

    @pl.when(sink)
    def _():
        arrived(kb.at[z, two], ryb)

    for d in order:
        send(kb.at[z, two], kb.at[z, two], rzb, (ylo * 8 + (z + d) % 8, sp))

    def forward(steps):
        for d in steps:
            there = (z + d) % 8

            @pl.when(source)
            def _():
                arrived(kb.at[there, one], rz.at[there])

            send(kb.at[there, one], kb.at[there, one], ry, across, source)

    forward(order[:4])

    for piece in range(4):
        @pl.when(x != piece)
        def _():
            arrived(wfb.at[core, :, piece], rwx.at[piece])
    send(wfb.at[core], wfb.at[core], rwc, partner)

    forward(order[4:])

    @pl.when(sink)
    def _():
        arrived(kb.at[:, one], ry)

    arrived(kb.at[pl.ds(0, 7), two], rzb)

    group = iota((8, 16, 128), 2) // 16
    for k in range(9):
        main, last = [], []
        for h in range(2):
            t = 2 * k + h
            main.append(kb[:, t])
            packed = kb[:, 18 + t // 8]
            last.append(jnp.where(group == t % 8, packed, jnp.zeros_like(packed)))
        pieces = []
        for zz in range(8):
            for h in range(2):
                pieces.append(jnp.concatenate([main[h][zz], last[h][zz]], axis=1))
        rhs[pl.ds(k * 256, 256), :] = jnp.concatenate(pieces, axis=0)

    zacc[...] = jnp.dot(sx[...], rhs[...], preferred_element_type=F32)

    field, corner = zacc[:, :128], zacc[:, 128:]
    column = iota((640, 128), 0) % 64
    g8 = iota((640, 128), 1) // 16
    tap_r, tap_c = g8 // 3, g8 % 3
    minus = jnp.where(column == 63, 0.0, pltpu.roll(field, 639, axis=0))
    plus = jnp.where(column == 0, 0.0, pltpu.roll(field, 1, axis=0))
    corner = jnp.where(column == 0, 0.0, pltpu.roll(corner, 1, axis=0))
    moved = jnp.where(tap_c == 0, minus, jnp.where(tap_c == 1, field, plus))
    none = jnp.zeros((64, 128), F32)
    total = jnp.concatenate([jnp.where(tap_r == 0, moved, 0.0), none, none], axis=0)
    total += jnp.concatenate([none, jnp.where(tap_r == 1, moved, 0.0), none], axis=0)
    total += jnp.concatenate([none, none, jnp.where(tap_r == 2, moved, 0.0) + corner], axis=0)
    total += pltpu.roll(total, 64, axis=1)
    total += pltpu.roll(total, 32, axis=1)
    total += pltpu.roll(total, 16, axis=1)
    lat[...] = total * (1.0 / 1.5305)
    g4 = (iota((32, 128), 1) // 16) % 4
    left16 = iota((16, 128), 1) < 64

    def unpack(packed):
        swapped = pltpu.roll(packed, 64, axis=1)
        return jnp.concatenate([jnp.where(left16, packed, swapped), jnp.where(left16, swapped, packed)], axis=0)

    for r in (0, 5, 1, 2, 3, 4):
        value = jnp.zeros((32, 128), F32)
        for p in range(2):
            for s in range(2):
                value = jnp.where(g4 == 2 * p + s, lat[pl.ds((2 * r + p) * 64 + s, 32, stride=2), :], value)
        if r == 0:
            edge[0] = jnp.where(left16, value[:16], value[16:])
        elif r == 5:
            edge[1] = jnp.where(left16, value[:16], value[16:])
            for c in range(2):
                send(edge.at[0], halo.at[1, core], rhd, (mem, jnp.maximum(2 * j - 2 + c, 0)), j > 0)
                send(edge.at[1], halo.at[0, core], rhu, (mem, jnp.minimum(2 * j + 2 + c, 31)), j < 15)
        else:
            tp[pl.ds((r - 1) * 32, 32), :] = value

    send(tp, tpr, rt, partner)

    @pl.when(j == 0)
    def _():
        halo[0] = jnp.zeros((2, 16, 128), F32)

    @pl.when(j == 15)
    def _():
        halo[1] = jnp.zeros((2, 16, 128), F32)

    arrived(wfb.at[0], rwc)
    for k in range(16):
        for c in range(2):
            block = wfb[c, k // 4, k % 4].astype(F32)
            at = 76 * (2 * k + c)
            wff[pl.ds(at, 40), :] = jnp.where(left, block, 0.0)[:40]
            wff[pl.ds(at + 38, 40), :] = jnp.where(left, pltpu.roll(block, 64, axis=1), 0.0)[:40]

    whole[...] = wff[pl.ds(0, 2432), :].astype(BF16)
    arrived(tpr, rt)

    @pl.when(j > 0)
    def _():
        arrived(halo.at[0], rhu)

    @pl.when(j < 15)
    def _():
        arrived(halo.at[1], rhd)

    above, below = unpack(halo[0, 0] + halo[0, 1]), unpack(halo[1, 0] + halo[1, 1])
    borders = jnp.concatenate([above, jnp.zeros((64, 128), F32), below], axis=0)
    gtd[...] = (tp[...] + tpr[...] + borders).astype(BF16)

    gmod[...] = lax.dot_general(gtd[...], whole[...], (((1,), (1,)), ((), ())), preferred_element_type=F32)
    line = jnp.sum(gmod[...] * nrm[...], axis=0, keepdims=True)
    low = [line[:, 128 * k : 128 * k + 128] for k in range(19)]
    low_rows = jnp.concatenate([pltpu.roll(low[9], 64, axis=1)] + low[:9], axis=0)
    high_rows = jnp.concatenate(low[9:], axis=0)
    shares = jnp.where(core == 0, low_rows, high_rows)

    prod = jnp.dot(nt2[...], gtd[...], preferred_element_type=F32).reshape(32, 48, 128)
    share = jnp.concatenate([jnp.zeros((38, 128), F32), shares], axis=0)
    spare = jnp.logical_or(row > 38, jnp.logical_and(row == 38, jnp.logical_not(left)))
    for k in range(16):
        nch[k] = jnp.where(spare, share, jnp.where(left, prod[2 * k], prod[2 * k + 1])).astype(BF16)
    for step in range(1, 16):
        there = (j + step) % 16
        send(nch.at[there], nrb.at[j], rn, (mem, there * 2 + core))
    nrb[j] = nch[j]

    mine = pl.ds(pl.multiple_of(core * 64, 64), 64)
    normed = nrm[mine, :]
    dn = gmod[mine, :] * (1.0 + scale)
    m1 = jnp.mean(dn, axis=-1, keepdims=True)
    m2 = jnp.mean(dn * normed, axis=-1, keepdims=True)
    ghv[...] = ((dn - m1 - normed * m2) * inv[mine, 0:1]).astype(BF16)
    out = pltpu.make_async_copy(ghv, gh_ref.at[0], lsem.at[0])
    out.start()
    flush()

    arrived(nrb.at[pl.ds(0, 15)], rn)
    member = jnp.sum(nrb[...].astype(F32), axis=0)

    tokens_sum = jnp.where(left[:1], member[38:39, :], pltpu.roll(member[38:39, :], 64, axis=1))
    cmb[...] = (own_scale * member + own_shift * tokens_sum).astype(BF16)
    for step in range(1, 16):
        send(cmb, mrb.at[mem], rm, ((mem + step) % 16, sp))
    mrb[mem] = cmb[...]

    gst[core] = jnp.concatenate([member[38:48], jnp.zeros((6, 128), F32)], axis=0)
    send(gst.at[core], gst.at[core], rgc, partner)
    high = tokens_sum.astype(BF16)
    low = (tokens_sum - high.astype(F32)).astype(BF16)
    pair = jnp.concatenate([high, low, jnp.zeros((14, 128), BF16)], axis=0)
    sums = lax.dot_general(pair, whole[...], (((1,), (1,)), ((), ())), preferred_element_type=F32)
    gsh_ref[...] = sums[0:1] + sums[1:2]

    flush()
    arrived(gst.at[0], rgc)
    middle = jnp.where(left[:1], pltpu.roll(gst[0, 0:1, :], 64, axis=1), gst[1, 0:1, :])
    gs_ref[...] = jnp.concatenate(
        [gst[0, k : k + 1, :] for k in range(1, 10)] + [middle] + [gst[1, k : k + 1, :] for k in range(1, 10)], axis=1)

    arrived(mrb.at[pl.ds(0, 15)], rm)
    final = jnp.sum(mrb[...].astype(F32), axis=0)
    square = jnp.concatenate([final, jnp.zeros((80, 128), F32)], axis=0).T
    lane = iota((64, 128), 1)
    out.wait()
    gf_ref[...] = jnp.where(lane < 38, square[:64], pltpu.roll(square[64:], 38, axis=1))[:, :76]


def place(*refs):
    ins, outs, held, sems = refs[:4], refs[4:8], refs[8:12], refs[12]
    reads = [pltpu.make_async_copy(ins[k], held[k], sems.at[k]) for k in range(4)]
    writes = [pltpu.make_async_copy(held[k], outs[k], sems.at[4 + k]) for k in range(4)]
    for copy in reads:
        copy.start()
    for k in (1, 2, 3, 0):
        reads[k].wait()
        writes[k].start()
    for copy in writes:
        copy.wait()


def per_device(grad_image, conv_weight, input_weight, hidden, shift, scale, final_weight):
    vmem = pl.BlockSpec(memory_space=pltpu.VMEM)
    hbm = pl.BlockSpec(memory_space=pl.ANY)
    dma = pltpu.SemaphoreType.DMA
    grad_hidden, grad_final, grad_scale, grad_shift = pl.pallas_call(
        kernel,
        out_shape=(
            jax.ShapeDtypeStruct((1, 64, 2432), BF16),
            jax.ShapeDtypeStruct((64, 76), F32),
            jax.ShapeDtypeStruct((1, 2432), F32),
            jax.ShapeDtypeStruct((1, 2432), F32),
        ),
        in_specs=[hbm] * 7,
        out_specs=(hbm, vmem, vmem, vmem),
        scratch_shapes=[
            pltpu.VMEM((9, 16, 32), BF16),
            pltpu.VMEM((144, 16), BF16),
            pltpu.VMEM((1, 2432), F32),
            pltpu.VMEM((1, 2432), F32),
            pltpu.VMEM((64, 76), BF16),
            pltpu.VMEM((16, 128, 256), BF16),
            pltpu.VMEM((2, 64, 2432), BF16),
            pltpu.VMEM((8, 128, 256), BF16),
            pltpu.VMEM((16, 512), BF16),
            pltpu.VMEM((32, 16, 512), BF16),
            pltpu.VMEM((8, 21, 16, 128), BF16),
            pltpu.VMEM((640, 2304), BF16),
            pltpu.VMEM((2, 144, 128), F32),
            pltpu.VMEM((2304, 256), BF16),
            pltpu.VMEM((640, 256), F32),
            pltpu.VMEM((768, 128), F32),
            pltpu.VMEM((128, 128), F32),
            pltpu.VMEM((128, 128), F32),
            pltpu.VMEM((2, 16, 128), F32),
            pltpu.VMEM((2, 2, 16, 128), F32),
            pltpu.VMEM((2, 4, 4, 48, 128), BF16),
            pltpu.VMEM((2440, 128), F32),
            pltpu.VMEM((2432, 128), BF16),
            pltpu.VMEM((128, 2432), F32),
            pltpu.VMEM((128, 128), F32),
            pltpu.VMEM((2448, 128), F32),
            pltpu.VMEM((1536, 128), BF16),
            pltpu.VMEM((128, 128), BF16),
            pltpu.VMEM((16, 48, 128), BF16),
            pltpu.VMEM((16, 48, 128), BF16),
            pltpu.VMEM((128, 2432), F32),
            pltpu.VMEM((64, 2432), BF16),
            pltpu.VMEM((2, 16, 128), F32),
            pltpu.VMEM((48, 128), BF16),
            pltpu.VMEM((16, 48, 128), BF16),
            dma((128,)),
            dma((8,)),
            dma, dma((8,)), dma, dma, dma,
            dma, dma, dma, dma,
            dma((4,)), dma((4,)), dma,
            dma, dma, dma, dma,
        ],
        compiler_params=pltpu.CompilerParams(
            collective_id=0, has_side_effects=True, vmem_limit_bytes=56 * 1024 * 1024
        ),
        cost_estimate=pl.CostEstimate(flops=1_000_000_000, bytes_accessed=2_000_000, transcendentals=0),
    )(
        grad_image,
        conv_weight.reshape(9, 16, 32),
        input_weight.reshape(144, 16),
        hidden,
        shift,
        scale,
        final_weight.T,
    )
    results = (grad_hidden, grad_final, grad_scale, grad_shift)
    grad_hidden, grad_final, grad_scale, grad_shift = pl.pallas_call(
        place,
        out_shape=tuple(jax.ShapeDtypeStruct(array.shape, array.dtype) for array in results),
        in_specs=[hbm] * 4,
        out_specs=(hbm,) * 4,
        scratch_shapes=[pltpu.VMEM(array.shape, array.dtype) for array in results] + [dma((8,))],
        compiler_params=pltpu.CompilerParams(vmem_limit_bytes=56 * 1024 * 1024),
    )(*results)
    return grad_hidden, grad_final.T, grad_scale, grad_shift


def solution(mesh):
    placed = (
        P("mem", "sp", None, None),
        P(None, None, "sp", "mem"),
        P(None, None, None, "sp"),
        P("mem", "sp", None),
        P("mem", None),
        P("mem", None),
        P("sp", None),
    )
    return jax.shard_map(
        per_device,
        mesh=mesh,
        in_specs=placed,
        out_specs=(P("mem", "sp", None), P("sp", None), P("mem", None), P("mem", None)),
        check_vma=False,
    )
```

time: 81.5 us -> 65.7 us (0.81)
  local copies, waits for them, and re-layouts: 7.8 us -> 0 us
  Pallas kernels: 72.1 us -> 64.9 us
    pallas_call x1, Pallas kernels: 72.1 us -> 63.2 us  [per_device(): pl.pallas_call(kernel, out_shape=(jax.ShapeDtypeStruct((1, 64, 2432), BF1...]
    unnamed x16 -> x0, local copies, waits for them, and re-layouts: 7.1 us -> none
    pallas_call x0 -> x1, Pallas kernels: none -> 1.76 us  [per_device(): pl.pallas_call(place, out_shape=tuple((jax.ShapeDtypeStruct(array.shape,...]
where the time goes in v2:
time: 65.7 us; the launch traced here: 65.6 us
  Pallas kernels  64.9 us (99%)
    pallas_call x1, Pallas kernels, per_device(): pl.pallas_call(kernel, out_shape=(jax.ShapeDtypeStruct((1, 64, 2432), BF1...  63.2 us
    pallas_call x1, Pallas kernels, per_device(): pl.pallas_call(place, out_shape=tuple((jax.ShapeDtypeStruct(array.shape,...  1.76 us

profile of v2, /device:TPU:6, one launch (start us, length us, event | category | flops | bytes accessed | tf_op | source)
XLA Modules:
  0.0 65.6 jit_solution(12011941756264987369)
XLA Ops:
  0.6 63.2 %shard_map.102 = (bf16[1,64,2432]{2,1,0:T(8,128)(2,1)}, f32[64,76]{1,0:T(8,128)}, f32[1,2432]{1,0:T(1,128)}, f32[1,2432]{1,0:T(1,128)}) custom-call(bf16[1,8,128,512]{3,2,1,0:T(8,128)(2,1)} %g_hbm.1, bf16[9,16,32]{2,1,0:T(8,128)(2,1)} %bitcast.4, bf16[144,16]{1,0:T(8,128)(2,1)} %bitcast.5, bf16[1,64,2432]{2,1,0:T(8,128)(2,1)} %hid_hbm.1, ...), custom_call_target="tpu_custom_call" | custom-call | flops 1000000000 | bytes 2000000 | tf_op jit(solution)/shard_map/pallas_call | solution.py:418
  63.8 1.8 %shard_map.103 = (bf16[1,64,2432]{2,1,0:T(8,128)(2,1)}, f32[64,76]{1,0:T(8,128)}, f32[1,2432]{1,0:T(1,128)}, f32[1,2432]{1,0:T(1,128)}) custom-call(bf16[1,64,2432]{2,1,0:T(8,128)(2,1)} %get-tuple-element.12.refs_0_, f32[64,76]{1,0:T(8,128)} %get-tuple-element.13.refs_1_, f32[1,2432]{1,0:T(1,128)} %get-tuple-element.14.refs_2_, ...), custom_call_target="tpu_custom_call" | custom-call | tf_op jit(solution)/shard_map/pallas_call | solution.py:485

commit v3 on v2

--- a/solution.py
+++ b/solution.py
@@ -7,7 +7,7 @@
 
 MESH = pl.DeviceIdType.MESH
 F32, BF16 = jnp.float32, jnp.bfloat16
-SPLIT = 10
+SPLIT = 17
 
 
 def iota(shape, dim):
@@ -18,8 +18,8 @@
     g_hbm, cw_hbm, iw_hbm, hid_hbm, shift_hbm, scale_hbm, wf_hbm,
     gh_ref, gf_ref, gs_ref, gsh_ref,
     cwv, iwv, shv, scv, wfv,
-    gall, hall, gother, pk, raw, kb, sx, ps, rhs, zacc, lat, tp, tpr, edge, halo,
-    wfb, wff, whole, nrm, inv, ntf, nt2, gtd, nch, nrb, gmod, ghv, gst, cmb, mrb,
+    gall, hall, gother, pk, raw, kb, sx, ps, rhs, zacc, lat, tp, tpr,
+    wfb, wff, whole, nrm, inv, ntf, nt2, gtd, nch, nrb, gmod, ghv, gfv, gsv, gshv, gst, cmb, mrb,
     ssem, lsem, rraw, rz, rzb, ry, ryb, rg, rh, rhu, rhd, rwy, rwx, rwc, rt, rn, rgc, rm,
 ):
     mem, sp = lax.axis_index("mem"), lax.axis_index("sp")
@@ -72,12 +72,17 @@
         greet(((mem + step) % 16, sp))
         return carry
 
+    def beside(up):
+        there = (2 * yhi + ylo + jnp.where(up, 1, 7)) % 8
+        return ((there % 2) * 8 + z, ((there // 2) * 4 + x) * 2 + core)
+
     lax.fori_loop(1, 32, greet_sp, 0)
     lax.fori_loop(1, 16, greet_mem, 0)
+    greet(beside(ylo == 1))
 
     loads = [
         (cw_hbm, cwv), (iw_hbm, iwv), (wf_hbm, wfv), (shift_hbm, shv), (scale_hbm, scv),
-        (g_hbm.at[0, :, :, pl.ds(pl.multiple_of(core * 256, 256), 256)], gall.at[pl.ds(core * 8, 8)]),
+        (g_hbm.at[0, :, :, pl.ds(pl.multiple_of(core * 256, 256), 256)], gall.at[pl.ds(3 + core * 8, 8)]),
         (hid_hbm.at[0], hall.at[core]),
         (g_hbm.at[0, :, :, pl.ds(pl.multiple_of(other * 256, 256), 256)], gother),
     ]
@@ -97,7 +102,7 @@
     wide = jnp.concatenate([wide, jnp.zeros((10, 128), F32)], axis=0)
     wfb[core, yhi, x] = wide.astype(BF16)
 
-    pl.semaphore_wait(barrier, 46)
+    pl.semaphore_wait(barrier, 47)
 
     source = core == ylo
     for step in range(16):
@@ -118,7 +123,7 @@
     loads[6].wait()
     send(hall.at[core], hall.at[core], rh, partner)
     loads[7].wait()
-    send(gother, gall.at[pl.ds(core * 8, 8)], rg, partner)
+    send(gother, gall.at[pl.ds(3 + core * 8, 8)], rg, partner)
 
     loads[3].wait()
     loads[4].wait()
@@ -164,27 +169,28 @@
     def columns(start):
         return jnp.concatenate([ps.at[half][pl.ds(start, 64, stride=2), :] for half in range(2)], axis=1)
 
-    sx[pl.ds(0, 64), pl.ds(768, 1536)] = jnp.zeros((64, 1536), BF16)
-    sx[pl.ds(576, 64), pl.ds(0, 1536)] = jnp.zeros((64, 1536), BF16)
-    for r in range(-1, 16):
-        pair = gall[max(r, 0)].astype(F32)
-        if 0 <= r < 15:
-            pair += gall[r + 1].astype(F32)
-        for half in range(2):
-            ps[half, pl.ds(8, 128), :] = pair[:, 128 * half : 128 * half + 128]
-        before, even, odd, after = columns(7), columns(8), columns(9), columns(10)
-        sums = jnp.concatenate([odd + after, even + odd, before + even], axis=1)
-        if r % 2 == 0:
-            places = ((r // 2, 1),)
-        else:
-            places = (((r - 1) // 2, 0), ((r + 1) // 2, 2))
-        for i, a in places:
-            kept = sums
-            if i == -1:
-                kept = jnp.where(j > 0, sums, 0.0)
-            if i == 8:
-                kept = jnp.where(j < 15, sums, 0.0)
-            sx[pl.ds((i + 1) * 64, 64), pl.ds(a * 768, 768)] = kept.astype(BF16)
+    def windows(pairs):
+        for r in pairs:
+            pair = gall[r + 3].astype(F32) + gall[r + 4].astype(F32)
+            for half in range(2):
+                ps[half, pl.ds(8, 128), :] = pair[:, 128 * half : 128 * half + 128]
+            before, even, odd, after = columns(7), columns(8), columns(9), columns(10)
+            sums = jnp.concatenate([odd + after, even + odd, before + even], axis=1)
+            if r % 2 == 0:
+                places = ((r // 2, 1),)
+            else:
+                places = (((r - 1) // 2, 0), ((r + 1) // 2, 2))
+            for i, a in places:
+                if i < -1 or i > 8:
+                    continue
+                kept = sums
+                if i == -1:
+                    kept = jnp.where(j > 0, sums, 0.0)
+                if i == 8:
+                    kept = jnp.where(j < 15, sums, 0.0)
+                sx[pl.ds((i + 1) * 64, 64), pl.ds(a * 768, 768)] = kept.astype(BF16)
+
+    windows(range(0, 15))
 
     for piece in range(4):
         @pl.when(yhi != piece)
@@ -218,13 +224,28 @@
     send(kb.at[z, two], kb.at[z, two], ryb, across, source)
     for d in order:
         send(kb.at[z, one], kb.at[z, one], rz.at[z], (ylo * 8 + (z + d) % 8, sp), source)
-    send(kb.at[z, one], kb.at[z, one], ry, across, source)
+    send(kb.at[z, one], kb.at[z, one], ry, beside(z % 2 == 0), source)
+
+    last, first = jnp.logical_and(core == 1, j < 15), jnp.logical_and(core == 0, j > 0)
+    up, down = jnp.minimum(2 * j + 2, 30), jnp.maximum(2 * j - 2, 0)
+    send(gall.at[pl.ds(16, 3)], gall.at[pl.ds(0, 3)], rhu, (mem, up + 1), last)
+    send(gother.at[pl.ds(5, 3)], gall.at[pl.ds(0, 3)], rhu, (mem, up), last)
+    send(gall.at[pl.ds(3, 3)], gall.at[pl.ds(19, 3)], rhd, (mem, down), first)
+    send(gother.at[pl.ds(0, 3)], gall.at[pl.ds(19, 3)], rhd, (mem, down + 1), first)
+
+    @pl.when(j == 0)
+    def _():
+        gall[pl.ds(0, 3)] = jnp.zeros((3, 128, 256), BF16)
+
+    @pl.when(j == 15)
+    def _():
+        gall[pl.ds(19, 3)] = jnp.zeros((3, 128, 256), BF16)
 
     @pl.when(sink)
     def _():
         arrived(kb.at[z, two], ryb)
 
-    for d in order:
+    for d in reversed(order):
         send(kb.at[z, two], kb.at[z, two], rzb, (ylo * 8 + (z + d) % 8, sp))
 
     def forward(steps):
@@ -235,7 +256,7 @@
             def _():
                 arrived(kb.at[there, one], rz.at[there])
 
-            send(kb.at[there, one], kb.at[there, one], ry, across, source)
+            send(kb.at[there, one], kb.at[there, one], ry, beside(there % 2 == 0), source)
 
     forward(order[:4])
 
@@ -246,6 +267,16 @@
     send(wfb.at[core], wfb.at[core], rwc, partner)
 
     forward(order[4:])
+
+    @pl.when(j > 0)
+    def _():
+        arrived(gall.at[pl.ds(0, 3)], rhu)
+
+    @pl.when(j < 15)
+    def _():
+        arrived(gall.at[pl.ds(0, 3)], rhd)
+
+    windows((-3, -2, -1, 15, 16, 17))
 
     @pl.when(sink)
     def _():
@@ -277,45 +308,21 @@
     plus = jnp.where(column == 0, 0.0, pltpu.roll(field, 1, axis=0))
     corner = jnp.where(column == 0, 0.0, pltpu.roll(corner, 1, axis=0))
     moved = jnp.where(tap_c == 0, minus, jnp.where(tap_c == 1, field, plus))
-    none = jnp.zeros((64, 128), F32)
-    total = jnp.concatenate([jnp.where(tap_r == 0, moved, 0.0), none, none], axis=0)
-    total += jnp.concatenate([none, jnp.where(tap_r == 1, moved, 0.0), none], axis=0)
-    total += jnp.concatenate([none, none, jnp.where(tap_r == 2, moved, 0.0) + corner], axis=0)
+    row_r = tap_r[:512]
+    total = jnp.where(row_r == 0, moved[128:], jnp.where(row_r == 1, moved[64:576], moved[:512])) + corner[:512]
     total += pltpu.roll(total, 64, axis=1)
     total += pltpu.roll(total, 32, axis=1)
     total += pltpu.roll(total, 16, axis=1)
     lat[...] = total * (1.0 / 1.5305)
     g4 = (iota((32, 128), 1) // 16) % 4
-    left16 = iota((16, 128), 1) < 64
-
-    def unpack(packed):
-        swapped = pltpu.roll(packed, 64, axis=1)
-        return jnp.concatenate([jnp.where(left16, packed, swapped), jnp.where(left16, swapped, packed)], axis=0)
-
-    for r in (0, 5, 1, 2, 3, 4):
+    for r in range(4):
         value = jnp.zeros((32, 128), F32)
         for p in range(2):
             for s in range(2):
                 value = jnp.where(g4 == 2 * p + s, lat[pl.ds((2 * r + p) * 64 + s, 32, stride=2), :], value)
-        if r == 0:
-            edge[0] = jnp.where(left16, value[:16], value[16:])
-        elif r == 5:
-            edge[1] = jnp.where(left16, value[:16], value[16:])
-            for c in range(2):
-                send(edge.at[0], halo.at[1, core], rhd, (mem, jnp.maximum(2 * j - 2 + c, 0)), j > 0)
-                send(edge.at[1], halo.at[0, core], rhu, (mem, jnp.minimum(2 * j + 2 + c, 31)), j < 15)
-        else:
-            tp[pl.ds((r - 1) * 32, 32), :] = value
+        tp[pl.ds(r * 32, 32), :] = value
 
     send(tp, tpr, rt, partner)
-
-    @pl.when(j == 0)
-    def _():
-        halo[0] = jnp.zeros((2, 16, 128), F32)
-
-    @pl.when(j == 15)
-    def _():
-        halo[1] = jnp.zeros((2, 16, 128), F32)
 
     arrived(wfb.at[0], rwc)
     for k in range(16):
@@ -327,18 +334,7 @@
 
     whole[...] = wff[pl.ds(0, 2432), :].astype(BF16)
     arrived(tpr, rt)
-
-    @pl.when(j > 0)
-    def _():
-        arrived(halo.at[0], rhu)
-
-    @pl.when(j < 15)
-    def _():
-        arrived(halo.at[1], rhd)
-
-    above, below = unpack(halo[0, 0] + halo[0, 1]), unpack(halo[1, 0] + halo[1, 1])
-    borders = jnp.concatenate([above, jnp.zeros((64, 128), F32), below], axis=0)
-    gtd[...] = (tp[...] + tpr[...] + borders).astype(BF16)
+    gtd[...] = (tp[...] + tpr[...]).astype(BF16)
 
     gmod[...] = lax.dot_general(gtd[...], whole[...], (((1,), (1,)), ((), ())), preferred_element_type=F32)
     line = jnp.sum(gmod[...] * nrm[...], axis=0, keepdims=True)
@@ -382,20 +378,28 @@
     low = (tokens_sum - high.astype(F32)).astype(BF16)
     pair = jnp.concatenate([high, low, jnp.zeros((14, 128), BF16)], axis=0)
     sums = lax.dot_general(pair, whole[...], (((1,), (1,)), ((), ())), preferred_element_type=F32)
-    gsh_ref[...] = sums[0:1] + sums[1:2]
+    gshv[...] = sums[0:1] + sums[1:2]
+    out_gsh = pltpu.make_async_copy(gshv, gsh_ref, lsem.at[1])
+    out_gsh.start()
 
     flush()
     arrived(gst.at[0], rgc)
     middle = jnp.where(left[:1], pltpu.roll(gst[0, 0:1, :], 64, axis=1), gst[1, 0:1, :])
-    gs_ref[...] = jnp.concatenate(
+    gsv[...] = jnp.concatenate(
         [gst[0, k : k + 1, :] for k in range(1, 10)] + [middle] + [gst[1, k : k + 1, :] for k in range(1, 10)], axis=1)
 
+    out_gs = pltpu.make_async_copy(gsv, gs_ref, lsem.at[2])
+    out_gs.start()
     arrived(mrb.at[pl.ds(0, 15)], rm)
     final = jnp.sum(mrb[...].astype(F32), axis=0)
     square = jnp.concatenate([final, jnp.zeros((80, 128), F32)], axis=0).T
     lane = iota((64, 128), 1)
-    out.wait()
-    gf_ref[...] = jnp.where(lane < 38, square[:64], pltpu.roll(square[64:], 38, axis=1))[:, :76]
+    gfv[...] = jnp.where(lane < 38, square[:64], pltpu.roll(square[64:], 38, axis=1))[:, :76]
+    out_gf = pltpu.make_async_copy(gfv, gf_ref, lsem.at[3])
+    out_gf.start()
+    flush()
+    for copy in (out, out_gsh, out_gs, out_gf):
+        copy.wait()
 
 
 def place(*refs):
@@ -412,7 +416,6 @@
 
 
 def per_device(grad_image, conv_weight, input_weight, hidden, shift, scale, final_weight):
-    vmem = pl.BlockSpec(memory_space=pltpu.VMEM)
     hbm = pl.BlockSpec(memory_space=pl.ANY)
     dma = pltpu.SemaphoreType.DMA
     grad_hidden, grad_final, grad_scale, grad_shift = pl.pallas_call(
@@ -424,14 +427,14 @@
             jax.ShapeDtypeStruct((1, 2432), F32),
         ),
         in_specs=[hbm] * 7,
-        out_specs=(hbm, vmem, vmem, vmem),
+        out_specs=(hbm,) * 4,
         scratch_shapes=[
             pltpu.VMEM((9, 16, 32), BF16),
             pltpu.VMEM((144, 16), BF16),
             pltpu.VMEM((1, 2432), F32),
             pltpu.VMEM((1, 2432), F32),
             pltpu.VMEM((64, 76), BF16),
-            pltpu.VMEM((16, 128, 256), BF16),
+            pltpu.VMEM((22, 128, 256), BF16),
             pltpu.VMEM((2, 64, 2432), BF16),
             pltpu.VMEM((8, 128, 256), BF16),
             pltpu.VMEM((16, 512), BF16),
@@ -441,11 +444,9 @@
             pltpu.VMEM((2, 144, 128), F32),
             pltpu.VMEM((2304, 256), BF16),
             pltpu.VMEM((640, 256), F32),
-            pltpu.VMEM((768, 128), F32),
+            pltpu.VMEM((512, 128), F32),
             pltpu.VMEM((128, 128), F32),
             pltpu.VMEM((128, 128), F32),
-            pltpu.VMEM((2, 16, 128), F32),
-            pltpu.VMEM((2, 2, 16, 128), F32),
             pltpu.VMEM((2, 4, 4, 48, 128), BF16),
             pltpu.VMEM((2440, 128), F32),
             pltpu.VMEM((2432, 128), BF16),
@@ -458,6 +459,9 @@
             pltpu.VMEM((16, 48, 128), BF16),
             pltpu.VMEM((128, 2432), F32),
             pltpu.VMEM((64, 2432), BF16),
+            pltpu.VMEM((64, 76), F32),
+            pltpu.VMEM((1, 2432), F32),
+            pltpu.VMEM((1, 2432), F32),
             pltpu.VMEM((2, 16, 128), F32),
             pltpu.VMEM((48, 128), BF16),
             pltpu.VMEM((16, 48, 128), BF16),

time: 65.7 us -> 61 us (0.928)
  Pallas kernels: 64.9 us -> 60.2 us
    pallas_call x1, Pallas kernels: 63.2 us -> 58.4 us  [per_device(): pl.pallas_call(kernel, out_shape=(jax.ShapeDtypeStruct((1, 64, 2432), BF1...]
where the time goes in v3:
time: 61 us; the launch traced here: 60.8 us
  Pallas kernels  60.2 us (99%)
  between operations  0.64 us (1%)
    pallas_call x1, Pallas kernels, per_device(): pl.pallas_call(kernel, out_shape=(jax.ShapeDtypeStruct((1, 64, 2432), BF1...  58.4 us
    pallas_call x1, Pallas kernels, per_device(): pl.pallas_call(place, out_shape=tuple((jax.ShapeDtypeStruct(array.shape,...  1.76 us

profile of v3, /device:TPU:6, one launch (start us, length us, event | category | flops | bytes accessed | tf_op | source)
XLA Modules:
  0.0 60.8 jit_solution(10460227144805045659)
XLA Ops:
  0.6 58.4 %shard_map.102 = (bf16[1,64,2432]{2,1,0:T(8,128)(2,1)}, f32[64,76]{1,0:T(8,128)}, f32[1,2432]{1,0:T(1,128)}, f32[1,2432]{1,0:T(1,128)}) custom-call(bf16[1,8,128,512]{3,2,1,0:T(8,128)(2,1)} %g_hbm.1, bf16[9,16,32]{2,1,0:T(8,128)(2,1)} %bitcast.4, bf16[144,16]{1,0:T(8,128)(2,1)} %bitcast.5, bf16[1,64,2432]{2,1,0:T(8,128)(2,1)} %hid_hbm.1, ...), custom_call_target="tpu_custom_call" | custom-call | flops 1000000000 | bytes 2000000 | tf_op jit(solution)/shard_map/pallas_call | solution.py:421
  59.1 1.8 %shard_map.103 = (bf16[1,64,2432]{2,1,0:T(8,128)(2,1)}, f32[64,76]{1,0:T(8,128)}, f32[1,2432]{1,0:T(1,128)}, f32[1,2432]{1,0:T(1,128)}) custom-call(bf16[1,64,2432]{2,1,0:T(8,128)(2,1)} %get-tuple-element.12.refs_0_, f32[64,76]{1,0:T(8,128)} %get-tuple-element.13.refs_1_, f32[1,2432]{1,0:T(1,128)} %get-tuple-element.14.refs_2_, ...), custom_call_target="tpu_custom_call" | custom-call | tf_op jit(solution)/shard_map/pallas_call | solution.py:489

commit v4 on v3

--- a/solution.py
+++ b/solution.py
@@ -404,13 +404,17 @@
 
 def place(*refs):
     ins, outs, held, sems = refs[:4], refs[4:8], refs[8:12], refs[12]
-    reads = [pltpu.make_async_copy(ins[k], held[k], sems.at[k]) for k in range(4)]
-    writes = [pltpu.make_async_copy(held[k], outs[k], sems.at[4 + k]) for k in range(4)]
-    for copy in reads:
-        copy.start()
-    for k in (1, 2, 3, 0):
-        reads[k].wait()
-        writes[k].start()
+    views = [lambda ref: ref] * 3 + [lambda ref, k=k: ref.at[0, pl.ds(16 * k, 16)] for k in range(4)]
+    which = (1, 2, 3, 0, 0, 0, 0)
+    reads, writes = [], []
+    for n, (view, k) in enumerate(zip(views, which)):
+        reads.append(pltpu.make_async_copy(view(ins[k]), view(held[k]), sems.at[n]))
+        writes.append(pltpu.make_async_copy(view(held[k]), view(outs[k]), sems.at[7 + n]))
+    for n in (3, 4, 5, 6, 0, 1, 2):
+        reads[n].start()
+    for n in (3, 4, 5, 6, 0, 1, 2):
+        reads[n].wait()
+        writes[n].start()
     for copy in writes:
         copy.wait()
 
@@ -491,7 +495,7 @@
         out_shape=tuple(jax.ShapeDtypeStruct(array.shape, array.dtype) for array in results),
         in_specs=[hbm] * 4,
         out_specs=(hbm,) * 4,
-        scratch_shapes=[pltpu.VMEM(array.shape, array.dtype) for array in results] + [dma((8,))],
+        scratch_shapes=[pltpu.VMEM(array.shape, array.dtype) for array in results] + [dma((14,))],
         compiler_params=pltpu.CompilerParams(vmem_limit_bytes=56 * 1024 * 1024),
     )(*results)
     return grad_hidden, grad_final.T, grad_scale, grad_shift

time: 61 us -> 61.1 us (level)
  no operation moved by 1% of the time
where the time goes in v4:
time: 61.1 us; the launch traced here: 60.8 us
  Pallas kernels  60.2 us (99%)
  between operations  0.64 us (1%)
    pallas_call x1, Pallas kernels, per_device(): pl.pallas_call(kernel, out_shape=(jax.ShapeDtypeStruct((1, 64, 2432), BF1...  58.4 us
    pallas_call x1, Pallas kernels, per_device(): pl.pallas_call(place, out_shape=tuple((jax.ShapeDtypeStruct(array.shape,...  1.77 us

profile of v4, /device:TPU:6, one launch (start us, length us, event | category | flops | bytes accessed | tf_op | source)
XLA Modules:
  0.0 60.8 jit_solution(6310814339718228184)
XLA Ops:
  0.6 58.4 %shard_map.102 = (bf16[1,64,2432]{2,1,0:T(8,128)(2,1)}, f32[64,76]{1,0:T(8,128)}, f32[1,2432]{1,0:T(1,128)}, f32[1,2432]{1,0:T(1,128)}) custom-call(bf16[1,8,128,512]{3,2,1,0:T(8,128)(2,1)} %g_hbm.1, bf16[9,16,32]{2,1,0:T(8,128)(2,1)} %bitcast.4, bf16[144,16]{1,0:T(8,128)(2,1)} %bitcast.5, bf16[1,64,2432]{2,1,0:T(8,128)(2,1)} %hid_hbm.1, ...), custom_call_target="tpu_custom_call" | custom-call | flops 1000000000 | bytes 2000000 | tf_op jit(solution)/shard_map/pallas_call | solution.py:425
  59.1 1.8 %shard_map.103 = (bf16[1,64,2432]{2,1,0:T(8,128)(2,1)}, f32[64,76]{1,0:T(8,128)}, f32[1,2432]{1,0:T(1,128)}, f32[1,2432]{1,0:T(1,128)}) custom-call(bf16[1,64,2432]{2,1,0:T(8,128)(2,1)} %get-tuple-element.12.refs_0_, f32[64,76]{1,0:T(8,128)} %get-tuple-element.13.refs_1_, f32[1,2432]{1,0:T(1,128)} %get-tuple-element.14.refs_2_, ...), custom_call_target="tpu_custom_call" | custom-call | tf_op jit(solution)/shard_map/pallas_call | solution.py:493
